TPU v7x, 32 devices: a whole 2x2x4 slice. The times are simulated.
32 devices in a mesh: member: 8 (over z, core), space: 4 (over y, x).
Axes of the slice: x: 2, y: 2, z: 4, core: 2. Of those that a mesh axis runs over, the one named last changes fastest.
Arguments:
- latents: bfloat16 [3072, 512], P('space'), may hold values from -6 to 6
- sample_perturbation: bfloat16 [24, 3072, 512], P('member', 'space'), may hold values from -6 to 6
- noise_table: float32 [64, 512], replicated, may hold values from 0.2 to 1.5
- member_seed: int32 [24], P('member'), may hold values from 0 to 63
- piece_arrangement: int32 [768], replicated, may hold values from 0 to 767, each once
- targets: bfloat16 [3072, 384], P('space'), may hold values from -4 to 4
- w_gate: bfloat16 [512, 1024], replicated, may hold values from -0.25 to 0.25
- w_up: bfloat16 [512, 1024], replicated, may hold values from -0.25 to 0.25
- lowering_matrix: bfloat16 [1024, 384], replicated, may hold values from -0.1875 to 0.1875
Outputs:
- latent_grad: float32 [3072, 512], P('space', 'member')
Inputs may be any that keep to these rules, and one draw needn't show every extreme that they name: `piece_arrangement`: a permutation of the 768 positions of a tile, the same for every tile.
All inputs are finite; a program needn't handle non-finite values.
Results may differ from a plain program's by a relative error of at most 0.0019.
Values may be sent and summed in bfloat16 or wider, within the bound.
A program may use at most 128 MiB of HBM per device.

v0:
```python
import functools

import jax
import jax.numpy as jnp
from jax import lax
from jax.experimental import pallas as pl
from jax.experimental.pallas import tpu as pltpu
from jax.sharding import PartitionSpec as P

PIECE_ITEMS = 8
ROWS = 16
LANES = 128
F32 = jnp.float32
BF16 = jnp.bfloat16


def dot(a, b, last=False):
    dims = (((1,), (1,)), ((), ())) if last else (((1,), (0,)), ((), ()))
    return lax.dot_general(a, b, dims, preferred_element_type=F32)


def three_way(x):
    high = x.astype(BF16)
    rest = x - high.astype(F32)
    mid = rest.astype(BF16)
    return high, mid, (rest - mid.astype(F32)).astype(BF16)


def kernel(
    n, own, chunks, block, hid_tile,
    seed_ref, arr_hbm, lat_hbm, table_hbm, pert_hbm, tgt_hbm, wg_hbm, wu_hbm, low_hbm,
    out_ref,
    arr_ref, lat_ref, table_ref, pert_ref, tgt_ref, wg_ref, wu_ref, low_ref,
    wg_t, wu_t, low_t,
    order, noisy, target, send, recv, hidden, gate_factor, up_factor, forecast, cotangent,
    grads, back_send, back_recv,
    load_sem, send_sem, recv_sem, back_send_sem, back_recv_sem,
):
    me = lax.axis_index("member")
    tokens, width = lat_ref.shape
    members = n * own
    hid = wg_ref.shape[1]
    result = low_ref.shape[1]
    scale = float(PIECE_ITEMS * result) ** 0.5
    far_first = sorted(range(1, n), key=lambda k: abs(k - n // 2))

    barrier = pltpu.get_barrier_semaphore()
    for k in range(1, n):
        pl.semaphore_signal(
            barrier, inc=1, device_id={"member": lax.rem(me + k, n)},
            device_id_type=pl.DeviceIdType.MESH,
        )
    loads = [
        pltpu.make_async_copy(src, dst, load_sem.at[i])
        for i, (src, dst) in enumerate(
            [(arr_hbm, arr_ref), (lat_hbm, lat_ref), (table_hbm, table_ref)]
            + [(pert_hbm.at[m], pert_ref.at[m]) for m in range(own)]
            + [(tgt_hbm, tgt_ref), (wg_hbm, wg_ref), (wu_hbm, wu_ref), (low_hbm, low_ref)]
        )
    ]
    for load in loads:
        load.start()

    def piece(c, d, s):
        return pltpu.make_async_remote_copy(
            src_ref=send.at[c, d],
            dst_ref=recv.at[c, pl.ds(s * own, own)],
            send_sem=send_sem.at[c, d],
            recv_sem=recv_sem.at[c, s],
            device_id={"member": d},
            device_id_type=pl.DeviceIdType.MESH,
        )

    def back_piece(c, d, s):
        return pltpu.make_async_remote_copy(
            src_ref=back_send.at[c, d],
            dst_ref=back_recv.at[s, c],
            send_sem=back_send_sem.at[c, d],
            recv_sem=back_recv_sem.at[s, c],
            device_id={"member": d},
            device_id_type=pl.DeviceIdType.MESH,
        )

    loads[0].wait()
    arr_row = arr_ref[...].reshape(1, tokens)
    arr_col = jnp.transpose(jnp.broadcast_to(arr_row, (8, tokens)))[:, :1]
    token = lax.broadcasted_iota(jnp.int32, (tokens, tokens), 1)
    picked = jnp.where(arr_col == token, 1.0, 0.0).astype(BF16)
    order[...] = picked.reshape(n, chunks, ROWS, tokens)
    loads[1].wait()
    loads[2].wait()
    row_of = lax.broadcasted_iota(jnp.int32, table_ref.shape, 0)
    latent = lat_ref[...].astype(F32)
    for m in range(own):
        loads[3 + m].wait()
        noise = jnp.sum(jnp.where(row_of == seed_ref[m], table_ref[...], 0.0), axis=0, keepdims=True)
        noisy[m] = (latent + pert_ref[m].astype(F32) * noise).astype(BF16)

    pl.semaphore_wait(barrier, n - 1)

    @pl.loop(0, chunks)
    def _(c):
        rows = order[:, c].reshape(n * ROWS, tokens)
        for m in range(own):
            send[c, :, m] = dot(rows, noisy[m]).astype(BF16).reshape(n, ROWS, width)
        for k in far_first:
            piece(c, lax.rem(me + k, n), me).start()
        recv[c, pl.ds(me * own, own)] = send[c, me]

    loads[3 + own].wait()
    target[...] = dot(order[me].reshape(chunks * ROWS, tokens), tgt_ref[...]).reshape(
        chunks, ROWS, result
    )
    for load in loads[4 + own :]:
        load.wait()
    wg_t[...] = jnp.transpose(wg_ref[...])
    wu_t[...] = jnp.transpose(wu_ref[...])
    low_t[...] = jnp.transpose(low_ref[...])

    def score(c):
        cells = members * PIECE_ITEMS
        left = lax.broadcasted_iota(jnp.int32, (cells, cells), 0)
        right = lax.broadcasted_iota(jnp.int32, (cells, cells), 1)
        same_item = left % PIECE_ITEMS == right % PIECE_ITEMS
        ones = jnp.where(left // PIECE_ITEMS == right // PIECE_ITEMS, 1.0, 0.0).astype(BF16)
        member_l = lax.broadcasted_iota(jnp.int32, (members, cells), 0)
        member_r = lax.broadcasted_iota(jnp.int32, (members, cells), 1)
        same_member = member_l == member_r // PIECE_ITEMS
        first_item = member_r % PIECE_ITEMS == 0
        for p in range(ROWS // PIECE_ITEMS):
            at = slice(p * PIECE_ITEMS, (p + 1) * PIECE_ITEMS)
            u3 = forecast[:, at, :]
            u = u3.reshape(cells, result)
            u16 = u.astype(BF16)
            products = jnp.where(same_item, dot(u16, u16, last=True), 0.0)
            by_item = jnp.sum(products.reshape(members, PIECE_ITEMS, cells), axis=1)
            gram = sum(dot(part, ones) for part in three_way(by_item))
            own_norm = jnp.sum(jnp.where(same_member & first_item, gram, 0.0), axis=1, keepdims=True)
            other_norm = jnp.sum(jnp.where(same_member, gram, 0.0), axis=0, keepdims=True)
            gap = jnp.where(same_member, 0.0, own_norm + other_norm - 2.0 * gram)
            weight = (1.0 / jnp.sqrt(gap + 1.0)).astype(BF16).astype(F32)
            total = jnp.sum(jnp.where(first_item, weight, 0.0), axis=1, keepdims=True)
            spread_out = jnp.broadcast_to(weight[:, None, :], (members, PIECE_ITEMS, cells))
            mixing = jnp.where(same_item, spread_out.reshape(cells, cells), 0.0).astype(BF16)
            weighted = dot(mixing, u16).reshape(members, PIECE_ITEMS, result)
            spread = (scale / members * (total[:, :, None] * u3 - weighted)).astype(BF16)
            miss = u3 - target[c, at, :][None]
            square = jnp.sum(miss * miss, axis=2, keepdims=True)
            norm = jnp.sqrt(jnp.sum(square, axis=1, keepdims=True) + 1.0)
            skill = miss / norm
            cotangent[:, at, :] = scale * skill - spread.astype(F32)

    @pl.loop(0, chunks)
    def _(c):
        for k in far_first:
            piece(c, me, lax.rem(me + k, n)).wait_recv()
        x = recv[c].reshape(members * ROWS, width)
        for h in range(0, hid, hid_tile):
            at = slice(h, h + hid_tile)
            gate = dot(x, wg_ref[:, at])
            up = dot(x, wu_ref[:, at])
            s = jax.nn.sigmoid(gate)
            gated = gate * s
            hidden[:, at] = (gated * up).astype(BF16)
            up_factor[:, at] = gated
            gate_factor[:, at] = up * (s + gated * (1.0 - s))
        value = dot(hidden[...], low_ref[...]).astype(BF16).astype(F32)
        forecast[...] = value.reshape(members, ROWS, result)
        score(c)
        ct = cotangent[...].reshape(members * ROWS, result).astype(BF16)
        for h in range(0, hid, hid_tile):
            at = slice(h, h + hid_tile)
            hidden_grad = dot(ct, low_t[:, at])
            for i, factor in enumerate((gate_factor, up_factor)):
                grad = (hidden_grad * factor[:, at]).astype(BF16).astype(F32)
                total = jnp.sum(grad.reshape(members, ROWS, hid_tile), axis=0)
                high = total.astype(BF16)
                grads[i, :ROWS, at] = high
                grads[i, ROWS:, at] = (total - high.astype(F32)).astype(BF16)
        y = dot(grads[0], wg_t[...]) + dot(grads[1], wu_t[...])
        y = y[:ROWS] + y[ROWS:]
        half = ROWS // 2
        for d in range(n):
            cols = slice(d * block, (d + 1) * block)
            parts = [y[:half, cols], y[half:, cols]]
            if 2 * block < LANES:
                parts.append(jnp.zeros((half, LANES - 2 * block), F32))
            back_send[c, d] = jnp.concatenate(parts, axis=1)
        for k in far_first:
            back_piece(c, lax.rem(me + k, n), me).start()
        back_recv[me, c] = back_send[c, me]

    @pl.loop(0, chunks)
    def _(c):
        for k in far_first:
            back_piece(c, me, lax.rem(me + k, n)).wait_recv()

    low_half = back_recv[...].reshape(n * chunks, 1, ROWS // 2, LANES)
    high_half = pltpu.roll(
        low_half.reshape(n * chunks * ROWS // 2, LANES), LANES - block, 1
    ).reshape(low_half.shape)
    patches = jnp.concatenate([low_half, high_half], axis=1).reshape(tokens, LANES)
    by_channel = jnp.transpose(patches)[:block]
    picks = order[...].reshape(tokens, tokens)
    out_ref[...] = sum(dot(part, picks) for part in three_way(by_channel))

    @pl.loop(0, chunks)
    def _(c):
        for k in far_first:
            d = lax.rem(me + k, n)
            piece(c, d, me).wait_send()
            back_piece(c, d, me).wait_send()


def body(
    latents, sample_perturbation, noise_table, member_seed, piece_arrangement, targets,
    w_gate, w_up, lowering_matrix,
):
    n = lax.axis_size("member")
    own = sample_perturbation.shape[0]
    tokens, width = latents.shape
    hid, result = lowering_matrix.shape
    members = n * own
    chunks = tokens // (n * ROWS)
    block = width // n
    assert 2 * block <= LANES and chunks * n * ROWS == tokens == piece_arrangement.shape[0]
    vmem = pl.BlockSpec(memory_space=pltpu.VMEM)
    smem = pl.BlockSpec(memory_space=pltpu.SMEM)
    hbm = pl.BlockSpec(memory_space=pl.ANY)
    half = ROWS // 2
    rows = members * ROWS
    return pl.pallas_call(
        functools.partial(kernel, n, own, chunks, block, 256),
        out_shape=jax.ShapeDtypeStruct((block, tokens), F32),
        in_specs=[smem] + [hbm] * 8,
        out_specs=vmem,
        scratch_shapes=[
            pltpu.VMEM(piece_arrangement.shape, jnp.int32),
            pltpu.VMEM(latents.shape, BF16),
            pltpu.VMEM(noise_table.shape, F32),
            pltpu.VMEM(sample_perturbation.shape, BF16),
            pltpu.VMEM(targets.shape, BF16),
            pltpu.VMEM(w_gate.shape, BF16),
            pltpu.VMEM(w_up.shape, BF16),
            pltpu.VMEM(lowering_matrix.shape, BF16),
            pltpu.VMEM((hid, width), BF16),
            pltpu.VMEM((hid, width), BF16),
            pltpu.VMEM((result, hid), BF16),
            pltpu.VMEM((n, chunks, ROWS, tokens), BF16),
            pltpu.VMEM((own, tokens, width), BF16),
            pltpu.VMEM((chunks, ROWS, result), F32),
            pltpu.VMEM((chunks, n, own, ROWS, width), BF16),
            pltpu.VMEM((chunks, members, ROWS, width), BF16),
            pltpu.VMEM((rows, hid), BF16),
            pltpu.VMEM((rows, hid), F32),
            pltpu.VMEM((rows, hid), F32),
            pltpu.VMEM((members, ROWS, result), F32),
            pltpu.VMEM((members, ROWS, result), F32),
            pltpu.VMEM((2, 2 * ROWS, hid), BF16),
            pltpu.VMEM((chunks, n, half, LANES), F32),
            pltpu.VMEM((n, chunks, half, LANES), F32),
            pltpu.SemaphoreType.DMA((7 + own,)),
            pltpu.SemaphoreType.DMA((chunks, n)),
            pltpu.SemaphoreType.DMA((chunks, n)),
            pltpu.SemaphoreType.DMA((chunks, n)),
            pltpu.SemaphoreType.DMA((n, chunks)),
        ],
        compiler_params=pltpu.CompilerParams(
            collective_id=0, has_side_effects=True, vmem_limit_bytes=64 * 1024 * 1024
        ),
        name="energy_score_gradient",
    )(
        member_seed, piece_arrangement, latents, noise_table, sample_perturbation,
        targets, w_gate, w_up, lowering_matrix,
    ).T


def solution(mesh):
    in_specs = (
        P("space", None),
        P("member", "space", None),
        P(),
        P("member"),
        P(),
        P("space", None),
        P(),
        P(),
        P(),
    )
    out_specs = P("space", "member")
    return jax.shard_map(body, mesh=mesh, in_specs=in_specs, out_specs=out_specs, check_vma=False)
```

profile of v0, /device:TPU:0, one launch (start us, length us, event | category | flops | bytes accessed | tf_op | source)
XLA Modules:
  0.0 72.7 jit_solution(433365138077444055)
XLA Ops:
  0.0 71.1 %energy_score_gradient.1 = f32[64,768]{1,0:T(8,128)} custom-call(s32[3]{0:T(128)} %seed_ref.1, s32[768]{0:T(1024)} %arr_hbm.1, bf16[768,512]{1,0:T(8,128)(2,1)} %lat_hbm.1, f32[64,512]{1,0:T(8,128)} %table_hbm.1, bf16[3,768,512]{2,1,0:T(8,128)(2,1)} %pert_hbm.1, bf16[768,384]{1,0:T(8,128)(2,1)} %tgt_hbm.1, bf16[512,1024]{1,0:T(8,128)(2,1)} %wg_hbm.1, ...), custom_call_target="tpu_custom_call" | custom-call | tf_op jit(solution)/shard_map/energy_score_gradient/pallas_call | solution.py:232
  71.1 1.6 %copy.11 = f32[768,64]{0,1:T(8,128)} copy(f32[768,64]{0,1:T(8,128)} %bitcast.1) | data formatting | bytes 393216
where the time goes:
time: 72.9 us; the launch traced here: 72.7 us
  Pallas kernels  71.1 us (98%)
  local copies, waits for them, and re-layouts  1.62 us (2%)
    pallas_call x1, Pallas kernels, body(): pl.pallas_call(functools.partial(kernel, n, own, chunks, block, 256), out...  71.1 us
    unnamed x1, local copies, waits for them, and re-layouts  1.62 us

commit v1 on v0

--- a/solution.py
+++ b/solution.py
@@ -10,6 +10,7 @@
 PIECE_ITEMS = 8
 ROWS = 16
 LANES = 128
+AHEAD = 2
 F32 = jnp.float32
 BF16 = jnp.bfloat16
 
@@ -98,14 +99,16 @@
 
     pl.semaphore_wait(barrier, n - 1)
 
-    @pl.loop(0, chunks)
-    def _(c):
+    def dispatch(c):
         rows = order[:, c].reshape(n * ROWS, tokens)
         for m in range(own):
             send[c, :, m] = dot(rows, noisy[m]).astype(BF16).reshape(n, ROWS, width)
         for k in far_first:
             piece(c, lax.rem(me + k, n), me).start()
         recv[c, pl.ds(me * own, own)] = send[c, me]
+
+    ahead = min(AHEAD, chunks)
+    pl.loop(0, ahead)(dispatch)
 
     loads[3 + own].wait()
     target[...] = dot(order[me].reshape(chunks * ROWS, tokens), tgt_ref[...]).reshape(
@@ -154,6 +157,11 @@
     def _(c):
         for k in far_first:
             piece(c, me, lax.rem(me + k, n)).wait_recv()
+
+        @pl.when(c + ahead < chunks)
+        def _():
+            dispatch(c + ahead)
+
         x = recv[c].reshape(members * ROWS, width)
         for h in range(0, hid, hid_tile):
             at = slice(h, h + hid_tile)
@@ -202,7 +210,7 @@
     patches = jnp.concatenate([low_half, high_half], axis=1).reshape(tokens, LANES)
     by_channel = jnp.transpose(patches)[:block]
     picks = order[...].reshape(tokens, tokens)
-    out_ref[...] = sum(dot(part, picks) for part in three_way(by_channel))
+    out_ref[...] = jnp.transpose(sum(dot(part, picks) for part in three_way(by_channel)))
 
     @pl.loop(0, chunks)
     def _(c):
@@ -231,7 +239,7 @@
     rows = members * ROWS
     return pl.pallas_call(
         functools.partial(kernel, n, own, chunks, block, 256),
-        out_shape=jax.ShapeDtypeStruct((block, tokens), F32),
+        out_shape=jax.ShapeDtypeStruct((tokens, block), F32),
         in_specs=[smem] + [hbm] * 8,
         out_specs=vmem,
         scratch_shapes=[
@@ -272,7 +280,7 @@
     )(
         member_seed, piece_arrangement, latents, noise_table, sample_perturbation,
         targets, w_gate, w_up, lowering_matrix,
-    ).T
+    )
 
 
 def solution(mesh):

time: 72.9 us -> 74.1 us (1.016)
  Pallas kernels: 71.1 us -> 72.1 us
    pallas_call x0 -> x1, local copies, waits for them, and re-layouts: none -> 1.82 us  [body(): pl.pallas_call(functools.partial(kernel, n, own, chunks, block, 256), out...]
    unnamed x1 -> x0, local copies, waits for them, and re-layouts: 1.62 us -> none
    pallas_call x1, Pallas kernels: 71.1 us -> 72.1 us  [body(): pl.pallas_call(functools.partial(kernel, n, own, chunks, block, 256), out...]
where the time goes in v1:
time: 74.1 us; the launch traced here: 73.9 us
  Pallas kernels  72.1 us (97%)
  local copies, waits for them, and re-layouts  1.82 us (2%)
    pallas_call x1, Pallas kernels, body(): pl.pallas_call(functools.partial(kernel, n, own, chunks, block, 256), out...  72.1 us
    pallas_call x1, local copies, waits for them, and re-layouts, body(): pl.pallas_call(functools.partial(kernel, n, own, chunks, block, 256), out...  1.82 us

profile of v1, /device:TPU:0, one launch (start us, length us, event | category | flops | bytes accessed | tf_op | source)
XLA Modules:
  0.0 73.9 jit_solution(11114509280458343809)
XLA Ops:
  0.0 72.1 %energy_score_gradient.1 = f32[768,64]{1,0:T(8,128)} custom-call(s32[3]{0:T(128)} %seed_ref.1, s32[768]{0:T(1024)} %arr_hbm.1, bf16[768,512]{1,0:T(8,128)(2,1)} %lat_hbm.1, f32[64,512]{1,0:T(8,128)} %table_hbm.1, bf16[3,768,512]{2,1,0:T(8,128)(2,1)} %pert_hbm.1, bf16[768,384]{1,0:T(8,128)(2,1)} %tgt_hbm.1, bf16[512,1024]{1,0:T(8,128)(2,1)} %wg_hbm.1, ...), custom_call_target="tpu_custom_call" | custom-call | tf_op jit(solution)/shard_map/energy_score_gradient/pallas_call | solution.py:240
  72.1 1.8 %copy.10 = f32[768,64]{0,1:T(8,128)} copy(f32[768,64]{1,0:T(8,128)} %energy_score_gradient.1) | data formatting | bytes 393216 | tf_op jit(solution)/shard_map/energy_score_gradient/pallas_call | solution.py:240

commit v2 on v1

--- a/solution.py
+++ b/solution.py
@@ -10,7 +10,6 @@
 PIECE_ITEMS = 8
 ROWS = 16
 LANES = 128
-AHEAD = 2
 F32 = jnp.float32
 BF16 = jnp.bfloat16
 
@@ -34,7 +33,7 @@
     arr_ref, lat_ref, table_ref, pert_ref, tgt_ref, wg_ref, wu_ref, low_ref,
     wg_t, wu_t, low_t,
     order, noisy, target, send, recv, hidden, gate_factor, up_factor, forecast, cotangent,
-    grads, back_send, back_recv,
+    grads, same_item, ones, same_member, back_send, back_recv,
     load_sem, send_sem, recv_sem, back_send_sem, back_recv_sem,
 ):
     me = lax.axis_index("member")
@@ -107,8 +106,7 @@
             piece(c, lax.rem(me + k, n), me).start()
         recv[c, pl.ds(me * own, own)] = send[c, me]
 
-    ahead = min(AHEAD, chunks)
-    pl.loop(0, ahead)(dispatch)
+    pl.loop(0, chunks)(dispatch)
 
     loads[3 + own].wait()
     target[...] = dot(order[me].reshape(chunks * ROWS, tokens), tgt_ref[...]).reshape(
@@ -120,54 +118,62 @@
     wu_t[...] = jnp.transpose(wu_ref[...])
     low_t[...] = jnp.transpose(low_ref[...])
 
+    cells = members * PIECE_ITEMS
+    left = lax.broadcasted_iota(jnp.int32, (cells, cells), 0)
+    right = lax.broadcasted_iota(jnp.int32, (cells, cells), 1)
+    same_item[...] = jnp.where((left & (PIECE_ITEMS - 1)) == (right & (PIECE_ITEMS - 1)), 1.0, 0.0)
+    ones[...] = jnp.where(left // PIECE_ITEMS == right // PIECE_ITEMS, 1.0, 0.0).astype(BF16)
+    member_l = lax.broadcasted_iota(jnp.int32, (members, cells), 0)
+    member_r = lax.broadcasted_iota(jnp.int32, (members, cells), 1)
+    same_member[...] = jnp.where(member_l == member_r // PIECE_ITEMS, 1.0, 0.0)
+
     def score(c):
-        cells = members * PIECE_ITEMS
-        left = lax.broadcasted_iota(jnp.int32, (cells, cells), 0)
-        right = lax.broadcasted_iota(jnp.int32, (cells, cells), 1)
-        same_item = left % PIECE_ITEMS == right % PIECE_ITEMS
-        ones = jnp.where(left // PIECE_ITEMS == right // PIECE_ITEMS, 1.0, 0.0).astype(BF16)
-        member_l = lax.broadcasted_iota(jnp.int32, (members, cells), 0)
-        member_r = lax.broadcasted_iota(jnp.int32, (members, cells), 1)
-        same_member = member_l == member_r // PIECE_ITEMS
-        first_item = member_r % PIECE_ITEMS == 0
-        for p in range(ROWS // PIECE_ITEMS):
-            at = slice(p * PIECE_ITEMS, (p + 1) * PIECE_ITEMS)
-            u3 = forecast[:, at, :]
-            u = u3.reshape(cells, result)
-            u16 = u.astype(BF16)
-            products = jnp.where(same_item, dot(u16, u16, last=True), 0.0)
-            by_item = jnp.sum(products.reshape(members, PIECE_ITEMS, cells), axis=1)
-            gram = sum(dot(part, ones) for part in three_way(by_item))
-            own_norm = jnp.sum(jnp.where(same_member & first_item, gram, 0.0), axis=1, keepdims=True)
-            other_norm = jnp.sum(jnp.where(same_member, gram, 0.0), axis=0, keepdims=True)
-            gap = jnp.where(same_member, 0.0, own_norm + other_norm - 2.0 * gram)
-            weight = (1.0 / jnp.sqrt(gap + 1.0)).astype(BF16).astype(F32)
-            total = jnp.sum(jnp.where(first_item, weight, 0.0), axis=1, keepdims=True)
-            spread_out = jnp.broadcast_to(weight[:, None, :], (members, PIECE_ITEMS, cells))
-            mixing = jnp.where(same_item, spread_out.reshape(cells, cells), 0.0).astype(BF16)
-            weighted = dot(mixing, u16).reshape(members, PIECE_ITEMS, result)
-            spread = (scale / members * (total[:, :, None] * u3 - weighted)).astype(BF16)
-            miss = u3 - target[c, at, :][None]
-            square = jnp.sum(miss * miss, axis=2, keepdims=True)
+        patches = [slice(p, p + PIECE_ITEMS) for p in range(0, ROWS, PIECE_ITEMS)]
+        us = [forecast[:, at, :].reshape(cells, result) for at in patches]
+        narrow = [u.astype(BF16) for u in us]
+        by_item = jnp.concatenate(
+            [
+                jnp.sum((dot(u, u, last=True) * same_item[...]).reshape(members, PIECE_ITEMS, cells), axis=1)
+                for u in narrow
+            ],
+            axis=0,
+        )
+        count = by_item.shape[0]
+        grams = dot(jnp.concatenate(three_way(by_item), axis=0), ones[...])
+        gram = (grams[:count] + grams[count : 2 * count] + grams[2 * count :]).reshape(
+            len(patches), members, cells
+        )
+        mine = same_member[...][None]
+        diagonal = gram * mine
+        own_norm = jnp.sum(diagonal, axis=2, keepdims=True) * (1.0 / PIECE_ITEMS)
+        other_norm = jnp.sum(diagonal, axis=1, keepdims=True)
+        gap = (own_norm + other_norm - 2.0 * gram) * (1.0 - mine)
+        weight = lax.rsqrt(gap + 1.0).astype(BF16).astype(F32)
+        for p, at in enumerate(patches):
+            u = us[p]
+            spread_out = jnp.broadcast_to(weight[p][:, None, :], (members, PIECE_ITEMS, cells))
+            mixing = spread_out.reshape(cells, cells) * same_item[...]
+            total = jnp.sum(mixing, axis=1, keepdims=True)
+            weighted = dot(mixing.astype(BF16), narrow[p])
+            spread = (scale / members * (total * u - weighted)).astype(BF16)
+            miss = (u.reshape(members, PIECE_ITEMS, result) - target[c, at, :][None]).reshape(u.shape)
+            square = jnp.sum(miss * miss, axis=1, keepdims=True).reshape(members, PIECE_ITEMS, 1)
             norm = jnp.sqrt(jnp.sum(square, axis=1, keepdims=True) + 1.0)
-            skill = miss / norm
-            cotangent[:, at, :] = scale * skill - spread.astype(F32)
+            per_norm = jnp.broadcast_to(scale / norm, square.shape).reshape(cells, 1)
+            cotangent[:, at, :] = (miss * per_norm - spread.astype(F32)).reshape(
+                members, PIECE_ITEMS, result
+            )
 
     @pl.loop(0, chunks)
     def _(c):
         for k in far_first:
             piece(c, me, lax.rem(me + k, n)).wait_recv()
-
-        @pl.when(c + ahead < chunks)
-        def _():
-            dispatch(c + ahead)
-
         x = recv[c].reshape(members * ROWS, width)
         for h in range(0, hid, hid_tile):
             at = slice(h, h + hid_tile)
             gate = dot(x, wg_ref[:, at])
             up = dot(x, wu_ref[:, at])
-            s = jax.nn.sigmoid(gate)
+            s = 0.5 * jnp.tanh(0.5 * gate) + 0.5
             gated = gate * s
             hidden[:, at] = (gated * up).astype(BF16)
             up_factor[:, at] = gated
@@ -265,6 +271,9 @@
             pltpu.VMEM((members, ROWS, result), F32),
             pltpu.VMEM((members, ROWS, result), F32),
             pltpu.VMEM((2, 2 * ROWS, hid), BF16),
+            pltpu.VMEM((members * PIECE_ITEMS, members * PIECE_ITEMS), F32),
+            pltpu.VMEM((members * PIECE_ITEMS, members * PIECE_ITEMS), BF16),
+            pltpu.VMEM((members, members * PIECE_ITEMS), F32),
             pltpu.VMEM((chunks, n, half, LANES), F32),
             pltpu.VMEM((n, chunks, half, LANES), F32),
             pltpu.SemaphoreType.DMA((7 + own,)),

time: 74.1 us -> 73 us (0.985)
  Pallas kernels: 72.1 us -> 71 us
    pallas_call x1, Pallas kernels: 72.1 us -> 71 us  [body(): pl.pallas_call(functools.partial(kernel, n, own, chunks, block, 256), out...]
where the time goes in v2:
time: 73 us; the launch traced here: 72.8 us
  Pallas kernels  71 us (97%)
  local copies, waits for them, and re-layouts  1.82 us (2%)
    pallas_call x1, Pallas kernels, body(): pl.pallas_call(functools.partial(kernel, n, own, chunks, block, 256), out...  71 us
    pallas_call x1, local copies, waits for them, and re-layouts, body(): pl.pallas_call(functools.partial(kernel, n, own, chunks, block, 256), out...  1.82 us

profile of v2, /device:TPU:0, one launch (start us, length us, event | category | flops | bytes accessed | tf_op | source)
XLA Modules:
  0.0 72.8 jit_solution(6212191364678749138)
XLA Ops:
  0.0 71.0 %energy_score_gradient.1 = f32[768,64]{1,0:T(8,128)} custom-call(s32[3]{0:T(128)} %seed_ref.1, s32[768]{0:T(1024)} %arr_hbm.1, bf16[768,512]{1,0:T(8,128)(2,1)} %lat_hbm.1, f32[64,512]{1,0:T(8,128)} %table_hbm.1, bf16[3,768,512]{2,1,0:T(8,128)(2,1)} %pert_hbm.1, bf16[768,384]{1,0:T(8,128)(2,1)} %tgt_hbm.1, bf16[512,1024]{1,0:T(8,128)(2,1)} %wg_hbm.1, ...), custom_call_target="tpu_custom_call" | custom-call | tf_op jit(solution)/shard_map/energy_score_gradient/pallas_call | solution.py:246
  71.0 1.8 %copy.10 = f32[768,64]{0,1:T(8,128)} copy(f32[768,64]{1,0:T(8,128)} %energy_score_gradient.1) | data formatting | bytes 393216 | tf_op jit(solution)/shard_map/energy_score_gradient/pallas_call | solution.py:246
